TPU v7x, 32 devices: a whole 2x2x4 slice. The times are simulated.
32 devices in a mesh: blk: 16 (over z, x, core), dim: 2 (over y).
Axes of the slice: x: 2, y: 2, z: 4, core: 2. Of those that a mesh axis runs over, the one named last changes fastest.
Arguments:
- points: bfloat16 [16384, 1024], P('blk', 'dim'), may hold values from -6 to 6
- owner: int32 [16384, 1], P('blk'), may hold values from 0 to 15; in each aligned block of 1024 rows (0 to 1023, 1024 to 2047, ...) at most 128 rows name the same one
- member: int32 [16384], P('blk'), may hold values from 0 to 8191
- centroids: bfloat16 [131072, 1024], P('blk', 'dim'), may hold values from -3 to 3
Outputs:
- new_centroids: bfloat16 [131072, 1024], P('blk', 'dim')
- nearest: float32 [16384], P('blk')
Inputs may be any that keep to these rules, and one draw needn't show every extreme that they name: In the rows of one index of blk, no owner value occurs more than 128 times, and some value occurs exactly 128 times.
All inputs are finite; a program needn't handle non-finite values.
Results may differ from a plain program's by a relative error of at most 0.0004.
Values may be sent and summed in bfloat16 or wider, within the bound.
A program may use at most 128 MiB of HBM per device.

v0:
```python
import jax
import jax.numpy as jnp
from jax import lax
from jax.sharding import PartitionSpec as P

D = 1024
CYCLE = 2


def passed_along(block, axis, distance):
    devices = range(lax.axis_size(axis))
    route = [((i - distance) % len(devices), i) for i in devices]
    return lax.ppermute(block, axis, route)


def block_least(full_points, point_squares, candidate):
    cand_floats = candidate.astype(jnp.float32)
    cand_squares = jnp.sum(cand_floats * cand_floats, axis=1)
    inner = lax.dot_general(
        full_points, candidate, (((1,), (1,)), ((), ())), preferred_element_type=jnp.float32
    )
    distance = (point_squares[:, None] + cand_squares[None, :] - 2.0 * inner) / D
    return jnp.min(distance, axis=1)


def row_squares(full_points):
    point_floats = full_points.astype(jnp.float32)
    return jnp.sum(point_floats * point_floats, axis=1)


def shards(points, owner, member, centroids):
    list_count = centroids.shape[0]
    half_width = centroids.shape[1]
    point_count = points.shape[0]
    block_count = lax.axis_size("blk")
    slot_count = 2 * point_count // block_count
    owners = owner[:, 0]
    one_hot = (owners[:, None] == jnp.arange(block_count, dtype=jnp.int32)[None, :]).astype(
        jnp.int32
    )
    earlier = jnp.cumsum(one_hot, axis=0) - one_hot
    position = jnp.sum(earlier * one_hot, axis=1)
    flat_slot = owners * slot_count + position
    send_rows = (
        jnp.zeros((block_count * slot_count, half_width), jnp.bfloat16).at[flat_slot].set(points)
    )
    send_index = (
        jnp.full((block_count * slot_count,), list_count, jnp.int32).at[flat_slot].set(member)
    )
    got_rows, got_index = (
        lax.all_to_all(
            send_rows.reshape(block_count, slot_count, half_width),
            "blk",
            split_axis=0,
            concat_axis=0,
            tiled=True,
        ),
        lax.all_to_all(
            send_index.reshape(block_count, slot_count),
            "blk",
            split_axis=0,
            concat_axis=0,
            tiled=True,
        ),
    )
    flat_index = got_index.reshape(-1)
    sums = (
        jnp.zeros((list_count, half_width), jnp.float32)
        .at[flat_index]
        .add(got_rows.reshape(-1, half_width).astype(jnp.float32), mode="drop")
    )
    counts = (
        jnp.zeros((list_count,), jnp.float32)
        .at[flat_index]
        .add(jnp.ones(flat_index.shape, jnp.float32), mode="drop")
    )
    new_centroids = ((sums + centroids.astype(jnp.float32)) / (counts[:, None] + 1.0)).astype(
        jnp.bfloat16
    )
    full_points = lax.all_gather(points, "dim", axis=1, tiled=True)
    point_squares = row_squares(full_points)
    best = jnp.full((point_count,), jnp.inf, jnp.float32)
    candidate = lax.all_to_all(new_centroids, "dim", split_axis=0, concat_axis=1, tiled=True)
    best = jnp.minimum(best, block_least(full_points, point_squares, candidate))
    visiting = full_points
    for section in range(1, CYCLE + 1):
        visiting = passed_along(visiting, "blk", -1)
        found = block_least(visiting, row_squares(visiting), candidate)
        returned = passed_along(found, "blk", section)
        best = jnp.minimum(best, returned)
    nearest = lax.pmin(best, "dim")
    return (new_centroids, nearest)


def solution(mesh):
    in_specs = (P("blk", "dim"), P("blk", None), P("blk"), P("blk", "dim"))
    out_specs = (P("blk", "dim"), P("blk"))
    return jax.shard_map(shards, mesh=mesh, in_specs=in_specs, out_specs=out_specs, check_vma=False)
```

profile of v0, /device:TPU:1, one launch (start us, length us, event | category | flops | bytes accessed | tf_op | source)
XLA Modules:
  0.0 316.3 jit_solution(6623979618736119740)
XLA Ops:
  7.9 4.5 %reduce-window.6 = s32[16,8,128]{2,1,0:T(8,128)S(1)} reduce-window(s32[16,8,128]{2,1,0:T(8,128)S(1)} %fusion.13, s32[]{:T(128)} %constant.12.clone.1), window={size=1x1x128 pad=0_0x0_0x127_0}, to_apply=%region_0.0 | reduce-window | flops 2080768 | bytes 131076 | tf_op jit(solution)/shard_map/reduce-window
  14.2 5.0 %scatter_custom_fusion = s32[2048]{0:T(1024)} fusion(s32[1024]{0:T(1024)S(1)} %bitcast.68, s32[1024]{0:T(1024)} %param.6, s32[]{:T(128)} %constant.10.clone.1), kind=kCustom, calls=%fused_computation.35 | custom fusion | bytes 8704 | tf_op jit(solution)/shard_map/scatter | solution.py:48
  19.2 7.3 %all-to-all-start = ((s32[16,1,128]{2,1,0:T(1,128)}), s32[16,1,128]{2,1,0:T(1,128)S(1)}, u32[]{:S(2)}, u32[]{:S(2)}) async-start(s32[16,1,128]{2,1,0:T(1,128)} %bitcast.6), calls=%async_computation | async-start | bytes 16384 | tf_op jit(solution)/shard_map/all_to_all | solution.py:58
  26.6 7.2 %scatter_custom_fusion.1 = bf16[2048,512]{1,0:T(8,128)(2,1)} fusion(s32[1024]{0:T(1024)S(1)} %bitcast.69, bf16[1024,512]{1,0:T(8,128)(2,1)} %param.4, bf16[]{:T(256)} %constant.14.clone.1), kind=kCustom, calls=%fused_computation.20 | custom fusion | bytes 2097664 | tf_op jit(solution)/shard_map/scatter | solution.py:45
  33.7 6.0 %all-to-all-start.1 = ((bf16[16,128,512]{2,1,0:T(8,128)(2,1)}), bf16[16,128,512]{2,1,0:T(8,128)(2,1)S(1)}, u32[]{:S(2)}, u32[]{:S(2)}) async-start(bf16[16,128,512]{2,1,0:T(8,128)(2,1)} %bitcast.60), calls=%async_computation.1 | async-start | bytes 4194304 | tf_op jit(solution)/shard_map/all_to_all | solution.py:51
  40.5 12.4 %convert_element_type.34 = f32[8192,512]{1,0:T(8,128)} convert(bf16[8192,512]{1,0:T(8,128)(2,1)} %param.7) | non-fusion elementwise | flops 4194304 | bytes 25165824 | tf_op jit(solution)/shard_map/convert_element_type | solution.py:77
  52.9 11.3 %scatter_custom_fusion.3 = f32[8192]{0:T(1024)S(1)} fusion(s32[2048]{0:T(1024)S(1)} %bitcast.66, f32[2048]{0:T(1024)S(1)} %broadcast.76, f32[]{:T(128)} %constant.15.clone.1), kind=kCustom, calls=%fused_computation.32 | custom fusion | flops 2048 | bytes 32772 | tf_op jit(solution)/shard_map/scatter-add | solution.py:75
  64.1 11.9 %all-gather.2.cloned.1.call-done = bf16[1024,1024]{1,0:T(8,128)(2,1)} async-done(((bf16[1024,512]{1,0:T(8,128)(2,1)}), bf16[1024,1024]{1,0:T(8,128)(2,1)}) %all-gather.2.cloned.1.call-update) | async-done | bytes 2097168 | tf_op jit(solution)/shard_map/all_gather | solution.py:80
  76.7 4.5 %all-to-all-done.1 = bf16[16,128,512]{2,1,0:T(8,128)(2,1)S(1)} async-done(((bf16[16,128,512]{2,1,0:T(8,128)(2,1)}), bf16[16,128,512]{2,1,0:T(8,128)(2,1)S(1)}, u32[]{:S(2)}, u32[]{:S(2)}) %all-to-all-start.1) | async-done | bytes 2097184 | tf_op jit(solution)/shard_map/all_to_all | solution.py:51
  81.2 24.3 %scatter_custom_fusion.2 = f32[8192,512]{1,0:T(8,128)} fusion(f32[8192,512]{1,0:T(8,128)} %convert_element_type.34, s32[2048]{0:T(1024)S(1)} %bitcast.67, bf16[2048,512]{1,0:T(8,128)(2,1)S(1)} %bitcast.59), kind=kCustom, calls=%fused_computation.15 | custom fusion | flops 2097152 | bytes 18874368 | tf_op jit(solution)/shard_map/scatter-add | solution.py:70
  105.5 9.1 %divide_convert_fusion = bf16[8192,512]{1,0:T(8,128)(2,1)} fusion(f32[8192,512]{1,0:T(8,128)} %scatter_custom_fusion.2, f32[8192]{0:T(1024)S(1)} %scatter_custom_fusion.3), kind=kLoop, calls=%fused_computation.14 | loop fusion | flops 8388608 | bytes 25198592 | tf_op jit(solution)/shard_map/convert_element_type | solution.py:77
  114.6 11.7 %copy.10 = bf16[2,4096,512]{1,2,0:T(8,128)(2,1)} copy(bf16[2,4096,512]{2,1,0:T(8,128)(2,1)} %bitcast.58) | data formatting | bytes 16777216 | tf_op jit(solution)/shard_map/all_to_all | solution.py:83
  126.3 7.1 %all-to-all-start.2 = ((bf16[2,4096,512]{1,2,0:T(8,128)(2,1)}), bf16[2,4096,512]{1,2,0:T(8,128)(2,1)}, u32[]{:S(2)}, u32[]{:S(2)}) async-start(bf16[2,4096,512]{1,2,0:T(8,128)(2,1)} %copy.10), calls=%async_computation.2 | async-start | bytes 16777216 | tf_op jit(solution)/shard_map/all_to_all | solution.py:83
  134.1 2.1 multiply_reduce_fusion.2
  136.2 24.5 %collective-permute-done.2 = bf16[1024,1024]{1,0:T(8,128)(2,1)S(1)} collective-permute-done((bf16[1024,1024]{1,0:T(8,128)(2,1)}, bf16[1024,1024]{1,0:T(8,128)(2,1)S(1)}, u32[]{:S(2)}, u32[]{:S(2)}) %collective-permute-start.2) | collective-permute-done | bytes 2097184 | tf_op jit(solution)/shard_map/ppermute | solution.py:13
  160.7 1.3 copy-done.1
  162.5 63.5 %all-to-all-done.2 = bf16[2,4096,512]{1,2,0:T(8,128)(2,1)} async-done(((bf16[2,4096,512]{1,2,0:T(8,128)(2,1)}), bf16[2,4096,512]{1,2,0:T(8,128)(2,1)}, u32[]{:S(2)}, u32[]{:S(2)}) %all-to-all-start.2) | async-done | bytes 8388640 | tf_op jit(solution)/shard_map/all_to_all | solution.py:83
  226.0 5.2 %multiply_reduce_fusion = f32[4096]{0:T(1024)S(1)} fusion(bf16[2,4096,512]{1,2,0:T(8,128)(2,1)} %all-to-all-done.2), kind=kLoop, calls=%fused_computation.13 | loop fusion | flops 12578816 | bytes 8404992 | tf_op jit(solution)/shard_map/reduce_sum | solution.py:18
  231.2 13.9 %fusion.1 = f32[1024]{0:T(1024)S(1)} fusion(bf16[4096,1024]{0,1:T(8,128)(2,1)} %bitcast.13, bf16[1024,1024]{1,0:T(8,128)(2,1)S(1)} %copy-done.2, f32[1024]{0:T(1024)S(1)} %multiply_reduce_fusion.1, f32[4096]{0:T(1024)S(1)} %multiply_reduce_fusion), kind=kOutput, calls=%fused_computation.6 | convolution fusion | flops 8610905088 | bytes 10510336 | tf_op jit(solution)/shard_map/dot_general | solution.py:19
  245.1 3.4 %collective-permute-start.3 = (f32[1024]{0:T(1024)S(1)}, f32[1024]{0:T(1024)S(1)}, u32[]{:S(2)}, u32[]{:S(2)}) collective-permute-start(f32[1024]{0:T(1024)S(1)} %fusion.1), channel_id=1, source_target_pairs={{28,0},{30,2},{0,4},{2,6},{4,8},{6,10},{8,12},{10,14},{12,16},{14,... | collective-permute-start | bytes 12296 | tf_op jit(solution)/shard_map/ppermute | solution.py:13
  248.5 15.8 %fusion.3 = f32[1024]{0:T(1024)S(1)} fusion(bf16[4096,1024]{0,1:T(8,128)(2,1)} %bitcast.13, bf16[1024,1024]{1,0:T(8,128)(2,1)} %collective-permute-done, f32[1024]{0:T(1024)S(1)} %multiply_reduce_fusion.2, f32[4096]{0:T(1024)S(1)} %multiply_reduce_fusion), kind=kOutput, calls=%fused_computation.9 | convolution fusion | flops 8610905088 | bytes 10510336 | tf_op jit(solution)/shard_map/dot_general | solution.py:19
  264.3 27.0 %collective-permute-start.1 = (f32[1024]{0:T(1024)S(1)}, f32[1024]{0:T(1024)S(1)}, u32[]{:S(2)}, u32[]{:S(2)}) collective-permute-start(f32[1024]{0:T(1024)S(1)} %fusion.3), channel_id=1, source_target_pairs={{30,0},{0,2},{2,4},{4,6},{6,8},{8,10},{10,12},{12,14},{14,16},{16,... | collective-permute-start | bytes 12296 | tf_op jit(solution)/shard_map/ppermute | solution.py:13
  291.3 13.8 %fusion.5 = f32[1024]{0:T(1024)S(1)} fusion(bf16[4096,1024]{0,1:T(8,128)(2,1)} %bitcast.13, bf16[1024,1024]{1,0:T(8,128)(2,1)S(1)} %copy-done, f32[4096]{0:T(1024)S(1)} %multiply_reduce_fusion, f32[1024]{0:T(1024)S(1)} %multiply_reduce_fusion.3), kind=kOutput, calls=%fused_computation.12 | convolution fusion | flops 8610905088 | bytes 10510336 | tf_op jit(solution)/shard_map/dot_general | solution.py:19
  305.1 4.4 %pmin.7 = f32[1024]{0:T(1024)} all-reduce(f32[1024]{0:T(1024)S(1)} %minimum_minimum_fusion), channel_id=1, replica_groups=mesh['blk'=16,'dim'=2] {'dim'}, use_global_device_ids=true, to_apply=%region_14.15 | all-reduce | flops 1024 | bytes 8192 | tf_op jit(solution)/shard_map/pmin | solution.py:91
  (27 shorter events, 5.1 us)
Async XLA Ops:
  19.2 14.5 %all-to-all-start = ((s32[16,1,128]{2,1,0:T(1,128)}), s32[16,1,128]{2,1,0:T(1,128)S(1)}, u32[]{:S(2)}, u32[]{:S(2)}) async-start(s32[16,1,128]{2,1,0:T(1,128)} %bitcast.6), calls=%async_computation | async-start | bytes 16384 | tf_op jit(solution)/shard_map/all_to_all | solution.py:58
  33.7 47.5 %all-to-all-start.1 = ((bf16[16,128,512]{2,1,0:T(8,128)(2,1)}), bf16[16,128,512]{2,1,0:T(8,128)(2,1)S(1)}, u32[]{:S(2)}, u32[]{:S(2)}) async-start(bf16[16,128,512]{2,1,0:T(8,128)(2,1)} %bitcast.60), calls=%async_computation.1 | async-start | bytes 4194304 | tf_op jit(solution)/shard_map/all_to_all | solution.py:51
  39.7 36.3 %all-gather.2.cloned.1.call-start = ((), (), s32[]{:S(2)}) async-start(), calls=%async_computation.3 | async-start | bytes 3145728 | tf_op jit(solution)/shard_map/all_gather | solution.py:80
  76.0 57.3 %collective-permute-start = (bf16[1024,1024]{1,0:T(8,128)(2,1)}, bf16[1024,1024]{1,0:T(8,128)(2,1)}, u32[]{:S(2)}, u32[]{:S(2)}) collective-permute-start(bf16[1024,1024]{1,0:T(8,128)(2,1)} %all-gather.2.cloned.1.call-done), channel_id=1, source_target_pairs={{2,0},{4,2},{6,4},{8,6},{10,8},{12,10},{14,12},{16,14},{18,16},{20... | collective-permute-start | bytes 6291464 | tf_op jit(solution)/shard_map/ppermute | solution.py:13
  126.3 7.3 %copy-start = (bf16[1024,1024]{1,0:T(8,128)(2,1)S(1)}, bf16[1024,1024]{1,0:T(8,128)(2,1)}, u32[]{:S(2)}) copy-start(bf16[1024,1024]{1,0:T(8,128)(2,1)} %all-gather.2.cloned.1.call-done) | copy-start | bytes 6291460
  126.3 99.6 %all-to-all-start.2 = ((bf16[2,4096,512]{1,2,0:T(8,128)(2,1)}), bf16[2,4096,512]{1,2,0:T(8,128)(2,1)}, u32[]{:S(2)}, u32[]{:S(2)}) async-start(bf16[2,4096,512]{1,2,0:T(8,128)(2,1)} %copy.10), calls=%async_computation.2 | async-start | bytes 16777216 | tf_op jit(solution)/shard_map/all_to_all | solution.py:83
  133.4 27.3 %collective-permute-start.2 = (bf16[1024,1024]{1,0:T(8,128)(2,1)}, bf16[1024,1024]{1,0:T(8,128)(2,1)S(1)}, u32[]{:S(2)}, u32[]{:S(2)}) collective-permute-start(bf16[1024,1024]{1,0:T(8,128)(2,1)} %collective-permute-done), channel_id=1, source_target_pairs={{2,0},{4,2},{6,4},{8,6},{10,8},{12,10},{14,12},{16,14},{18,16},{20... | collective-permute-start | bytes 6291464 | tf_op jit(solution)/shard_map/ppermute | solution.py:13
  160.7 1.3 copy-start.1
  226.0 5.2 %copy-start.2 = (bf16[1024,1024]{1,0:T(8,128)(2,1)S(1)}, bf16[1024,1024]{1,0:T(8,128)(2,1)}, u32[]{:S(2)}) copy-start(bf16[1024,1024]{1,0:T(8,128)(2,1)} %copy-done.1) | copy-start | bytes 6291460
  245.1 59.9 %collective-permute-start.3 = (f32[1024]{0:T(1024)S(1)}, f32[1024]{0:T(1024)S(1)}, u32[]{:S(2)}, u32[]{:S(2)}) collective-permute-start(f32[1024]{0:T(1024)S(1)} %fusion.1), channel_id=1, source_target_pairs={{28,0},{30,2},{0,4},{2,6},{4,8},{6,10},{8,12},{10,14},{12,16},{14,... | collective-permute-start | bytes 12296 | tf_op jit(solution)/shard_map/ppermute | solution.py:13
  264.3 40.8 %collective-permute-start.1 = (f32[1024]{0:T(1024)S(1)}, f32[1024]{0:T(1024)S(1)}, u32[]{:S(2)}, u32[]{:S(2)}) collective-permute-start(f32[1024]{0:T(1024)S(1)} %fusion.3), channel_id=1, source_target_pairs={{30,0},{0,2},{2,4},{4,6},{6,8},{8,10},{10,12},{12,14},{14,16},{16,... | collective-permute-start | bytes 12296 | tf_op jit(solution)/shard_map/ppermute | solution.py:13
Sparse Core Ops, SparseCore 0:
  42.1 33.8 all-gather.1
where the time goes:
time: 317 us; the launch traced here: 316 us
  waiting for transfers between devices  105 us (33%)
  other arithmetic  72 us (23%)
  starting transfers between devices  51.7 us (16%)
  matrix products  43.5 us (14%)
  local copies, waits for them, and re-layouts  25.5 us (8%)
  between operations  14.2 us (4%)
  blocking collectives  4.38 us (1%)
    all_to_all x1, waiting for transfers between devices, shards(): lax.all_to_all(new_centroids, 'dim', split_axis=0, concat_axis=1, tiled=T...  63.5 us
    dot_general x3, matrix products, block_least(): lax.dot_general(full_points, candidate, (((1,), (1,)), ((), ())), preferr...  43.5 us
    ppermute x4, starting transfers between devices, passed_along(): return lax.ppermute(block, axis, route)  31.3 us
    ppermute x4, waiting for transfers between devices, passed_along(): return lax.ppermute(block, axis, route)  24.5 us
    scatter-add x1, other arithmetic, shards(): sums = jnp.zeros((list_count, half_width), jnp.float32).at[flat_index].ad...  24.3 us
    convert_element_type x1, other arithmetic, shards(): centroids.astype(jnp.float32)  12.4 us
    all_gather x1, waiting for transfers between devices, shards(): full_points = lax.all_gather(points, 'dim', axis=1, tiled=True)  11.9 us
    all_to_all x1, local copies, waits for them, and re-layouts, shards(): lax.all_to_all(new_centroids, 'dim', split_axis=0, concat_axis=1, tiled=T...  11.7 us
  transfers between devices with their start and end apart: 8, of which 4 were waited for; matrix products, arithmetic and copies ran while one was open for 34% of the time, Pallas kernels for 0%

commit v1 on v0

v1 whole, which is shorter than its diff:
```python
import functools

import jax
import jax.numpy as jnp
from jax import lax
from jax.experimental import pallas as pl
from jax.experimental.pallas import tpu as pltpu
from jax.sharding import PartitionSpec as P

CYCLE = 2
LANES = 128
MESH = pl.DeviceIdType.MESH
NT = (((1,), (1,)), ((), ()))
F32, BF16, I32 = jnp.float32, jnp.bfloat16, jnp.int32


def kernel(
    n, slots, tile,
    owner_ref, member_ref, points_hbm, cent_hbm,
    new_hbm, near_ref,
    pts, cent, cand, send, recv, isend, irecv, idx_row, slot_row, mins, got, squares,
    load_sem, row_send, row_recv, ind_send, ind_recv, pt_send, pt_recv,
    ring_send, ring_recv, chunk_send, chunk_recv, out_sem, min_send, min_recv,
):
    rows, half = points_hbm.shape
    lists = cent_hbm.shape[0]
    keep = lists // 2
    chunks = keep // tile
    total = n * slots
    share = LANES // slots
    me, side = lax.axis_index("blk"), lax.axis_index("dim")
    other = 1 - side

    load_points = pltpu.make_async_copy(points_hbm, pts.at[0, :, pl.ds(0, half)], load_sem.at[0])
    load_points.start()
    load_cent = pltpu.make_async_copy(cent_hbm, cent, load_sem.at[1])
    load_cent.start()

    barrier = pltpu.get_barrier_semaphore()

    def greet(d, carry):
        pl.semaphore_signal(
            barrier, inc=1, device_id=(lax.rem(me + d, n), side), device_id_type=MESH)
        return carry

    lax.fori_loop(1, n, greet, 0)
    for s in range(-CYCLE, CYCLE + 1):
        pl.semaphore_signal(
            barrier, inc=1, device_id=(lax.rem(me + s + n, n), other), device_id_type=MESH)

    owner = owner_ref[...]
    owned = lax.broadcasted_iota(I32, (n, rows), 0) == owner
    before = lax.broadcasted_iota(I32, (rows, rows), 0) < lax.broadcasted_iota(I32, (rows, rows), 1)
    earlier = jnp.dot(
        owned.astype(F32).astype(BF16), before.astype(F32).astype(BF16), preferred_element_type=F32)
    rank = jnp.sum(jnp.where(owned, earlier, 0.0), axis=0, keepdims=True).astype(I32)
    slot_row[...] = jnp.broadcast_to(owner * slots + rank, slot_row.shape)

    code = member_ref[...] + 1
    shift = slots * lax.rem(me, share)
    lane_of = (lax.broadcasted_iota(I32, (LANES, rows), 0) == rank + shift).astype(F32).astype(BF16)
    high = jnp.where(owned, (code >> 7).astype(F32), 0.0).astype(BF16)
    low = jnp.where(owned, (code & 127).astype(F32), 0.0).astype(BF16)
    codes = 128.0 * lax.dot_general(high, lane_of, NT, preferred_element_type=F32)
    codes = codes + lax.dot_general(low, lane_of, NT, preferred_element_type=F32)
    codes = codes.astype(I32)
    for j in range(n):
        isend[j] = jnp.broadcast_to(codes[j:j + 1, :], isend.shape[1:])

    load_points.wait()
    pl.semaphore_wait(barrier, n - 1 + 2 * CYCLE + 1)

    own_pts = pts.at[0, :, pl.ds(0, half)]
    point_copy = pltpu.make_async_remote_copy(
        src_ref=own_pts, dst_ref=pts.at[0, :, pl.ds(half, half)],
        send_sem=pt_send, recv_sem=pt_recv, device_id=(me, other), device_id_type=MESH)
    point_copy.start()

    def pack(j):
        base = pl.multiple_of(j * slots, slots)
        place = lax.broadcasted_iota(I32, (slots, rows), 0) + base
        pick = (place == slot_row[0:1, :]).astype(F32).astype(BF16)
        packed = jnp.dot(pick, pts[0, :, 0:half], preferred_element_type=F32).astype(BF16)
        return base, packed

    def copies(d):
        j = lax.rem(me + d, n)
        there = pl.ds(pl.multiple_of(me * slots, slots), slots)
        row_copy = pltpu.make_async_remote_copy(
            src_ref=send.at[pl.ds(pl.multiple_of(j * slots, slots), slots)], dst_ref=recv.at[there],
            send_sem=row_send.at[d], recv_sem=row_recv.at[d],
            device_id=(j, side), device_id_type=MESH)
        ind_copy = pltpu.make_async_remote_copy(
            src_ref=isend.at[j], dst_ref=irecv.at[me],
            send_sem=ind_send.at[d], recv_sem=ind_recv.at[d],
            device_id=(j, side), device_id_type=MESH)
        return row_copy, ind_copy

    def dispatch(i, carry):
        d = 1 + lax.rem(i + n // 4, n - 1)
        base, packed = pack(lax.rem(me + d, n))
        send[pl.ds(base, slots), :] = packed
        row_copy, ind_copy = copies(d)
        ind_copy.start()
        row_copy.start()
        return carry

    lax.fori_loop(0, n - 1, dispatch, 0)
    base, packed = pack(me)
    recv[pl.ds(base, slots), :] = packed
    irecv[me] = isend[me]

    point_copy.wait()
    ones = jnp.ones((8, 2 * half), BF16)
    block = min(256, rows)
    for r in range(rows // block):
        p = pts[0, r * block:(r + 1) * block, :].astype(F32)
        sq = p * p
        top = sq.astype(BF16)
        rest = (sq - top.astype(F32)).astype(BF16)
        squares[:, r * block:(r + 1) * block] = lax.dot_general(
            ones, top, NT, preferred_element_type=F32
        ) + lax.dot_general(ones, rest, NT, preferred_element_type=F32)
    mins[...] = jnp.full(mins.shape, jnp.inf, F32)
    load_cent.wait()

    def arrive(d, carry):
        row_copy, ind_copy = copies(d)
        ind_copy.wait()
        row_copy.wait()
        return carry

    lax.fori_loop(1, n, arrive, 0)
    for g in range(total // LANES):
        line = irecv[g * share]
        for i in range(1, share):
            line = line + irecv[g * share + i]
        idx_row[:, g * LANES:(g + 1) * LANES] = line

    previous = lax.rem(me + n - 1, n)

    def ring(s):
        return pltpu.make_async_remote_copy(
            src_ref=pts.at[s - 1], dst_ref=pts.at[s],
            send_sem=ring_send.at[s - 1], recv_sem=ring_recv.at[s - 1],
            device_id=(previous, side), device_id_type=MESH)

    ring(1).start()

    def updated(first):
        number = lax.broadcasted_iota(I32, (tile, total), 0) + (first + 1)
        hot = (number == idx_row[0:1, :]).astype(F32)
        count = jnp.sum(hot, axis=1, keepdims=True)
        sums = jnp.dot(hot.astype(BF16), recv[...], preferred_element_type=F32)
        old = cent[pl.ds(first, tile), :].astype(F32)
        return ((sums + old) * (1.0 / (count + 1.0))).astype(BF16)

    def start_of(c, whose):
        return pl.multiple_of(whose * keep + c * tile, tile)

    def chunk_copy(c):
        return pltpu.make_async_remote_copy(
            src_ref=cent.at[pl.ds(start_of(c, other), tile)],
            dst_ref=cand.at[pl.ds(pl.multiple_of(c * tile, tile), tile), pl.ds(half, half)],
            send_sem=chunk_send.at[c], recv_sem=chunk_recv.at[c],
            device_id=(me, other), device_id_type=MESH)

    def sent_out(c):
        place = pl.ds(start_of(c, other), tile)
        return pltpu.make_async_copy(cent.at[place], new_hbm.at[place], out_sem.at[0, c])

    def kept_out(c):
        here = pl.ds(pl.multiple_of(c * tile, tile), tile)
        return pltpu.make_async_copy(
            cand.at[here, pl.ds(0, half)], new_hbm.at[pl.ds(start_of(c, side), tile)],
            out_sem.at[1, c])

    def give(c, carry):
        first = start_of(c, other)
        cent[pl.ds(first, tile), :] = updated(first)
        chunk_copy(c).start()
        sent_out(c).start()
        return carry

    lax.fori_loop(0, chunks, give, 0)
    for s in range(1, CYCLE):
        ring(s).wait_recv()
        ring(s + 1).start()

    def hold(c, carry):
        here = pl.ds(pl.multiple_of(c * tile, tile), tile)
        cand[here, 0:half] = updated(start_of(c, side))
        kept_out(c).start()
        return carry

    lax.fori_loop(0, chunks, hold, 0)
    ring(CYCLE).wait_recv()

    def search(c, carry):
        chunk_copy(c).wait_recv()
        block_c = cand[pl.ds(pl.multiple_of(c * tile, tile), tile), :]
        wide = block_c.astype(F32)
        half_square = 0.5 * jnp.sum(wide * wide, axis=1, keepdims=True)
        for s in range(CYCLE + 1):
            inner = lax.dot_general(block_c, pts[s], NT, preferred_element_type=F32)
            value = (half_square - inner).reshape(tile // 8, 8, rows)
            mins[s] = jnp.minimum(mins[s], jnp.min(value, axis=0))
        return carry

    lax.fori_loop(0, chunks, search, 0)

    back = []
    for s in range(CYCLE + 1):
        for way in range(2):
            if s == 0 and way == 0:
                continue
            back.append(pltpu.make_async_remote_copy(
                src_ref=mins.at[s], dst_ref=got.at[way, s],
                send_sem=min_send.at[way, s], recv_sem=min_recv.at[way, s],
                device_id=(lax.rem(me + s, n), other if way else side), device_id_type=MESH))
    for copy in back:
        copy.start()

    def finish(c, carry):
        chunk_copy(c).wait_send()
        sent_out(c).wait()
        kept_out(c).wait()
        return carry

    lax.fori_loop(0, chunks, finish, 0)
    for s in range(1, CYCLE + 1):
        ring(s).wait_send()
    for copy in back:
        copy.wait()
    best = mins[0]
    for s in range(CYCLE + 1):
        for way in range(2):
            if s or way:
                best = jnp.minimum(best, got[way, s])
    least = jnp.min(best, axis=0, keepdims=True)
    near_ref[...] = (squares[0:1, :] + 2.0 * least) / (2 * half)


def shards(points, owner, member, centroids):
    n = lax.axis_size("blk")
    rows, half = points.shape
    lists = centroids.shape[0]
    slots = 2 * rows // n
    tile = min(256, lists // 4)
    chunks = lists // 2 // tile
    total = n * slots
    anywhere, vmem = pl.BlockSpec(memory_space=pl.ANY), pl.BlockSpec(memory_space=pltpu.VMEM)
    dma = pltpu.SemaphoreType.DMA
    new, near = pl.pallas_call(
        functools.partial(kernel, n, slots, tile),
        out_shape=(
            jax.ShapeDtypeStruct(centroids.shape, BF16),
            jax.ShapeDtypeStruct((1, rows), F32),
        ),
        in_specs=[vmem, vmem, anywhere, anywhere],
        out_specs=(anywhere, vmem),
        scratch_shapes=[
            pltpu.VMEM((CYCLE + 1, rows, 2 * half), BF16),
            pltpu.VMEM((lists, half), BF16),
            pltpu.VMEM((lists // 2, 2 * half), BF16),
            pltpu.VMEM((total, half), BF16),
            pltpu.VMEM((total, half), BF16),
            pltpu.VMEM((n, 8, LANES), I32),
            pltpu.VMEM((n, 8, LANES), I32),
            pltpu.VMEM((8, total), I32),
            pltpu.VMEM((8, rows), I32),
            pltpu.VMEM((CYCLE + 1, 8, rows), F32),
            pltpu.VMEM((2, CYCLE + 1, 8, rows), F32),
            pltpu.VMEM((8, rows), F32),
            dma((2,)), dma((n,)), dma((n,)), dma((n,)), dma((n,)), dma, dma,
            dma((CYCLE,)), dma((CYCLE,)), dma((chunks,)), dma((chunks,)), dma((2, chunks)),
            dma((2, CYCLE + 1)), dma((2, CYCLE + 1)),
        ],
        compiler_params=pltpu.CompilerParams(
            collective_id=0, has_side_effects=True, vmem_limit_bytes=56 * 1024 * 1024),
    )(owner.reshape(1, rows), member.reshape(1, rows), points, centroids)
    return new, near.reshape(rows)


def solution(mesh):
    in_specs = (P("blk", "dim"), P("blk", None), P("blk"), P("blk", "dim"))
    out_specs = (P("blk", "dim"), P("blk"))
    return jax.shard_map(shards, mesh=mesh, in_specs=in_specs, out_specs=out_specs, check_vma=False)
```

time: 317 us -> 207 us (0.65)
  Pallas kernels: 0 us -> 198 us
  waiting for transfers between devices: 105 us -> 0 us
  other arithmetic: 72 us -> 0 us
  starting transfers between devices: 51.7 us -> 0 us
  matrix products: 43.5 us -> 0 us
  local copies, waits for them, and re-layouts: 25.5 us -> 7.92 us
  between operations: 14.2 us -> 0.65 us
  blocking collectives: 4.38 us -> 0 us
    pallas_call x0 -> x1, Pallas kernels: none -> 198 us  [shards(): pl.pallas_call(functools.partial(kernel, n, slots, tile), out_shape=(jax....]
    all_to_all x3 -> x0, waiting for transfers between devices: 68 us -> none  [the longest x1 63.5 us: shards(): lax.all_to_all(new_centroids, 'dim', split_axis=0, concat_axis=1, tiled=T...]
    dot_general x3 -> x0, matrix products: 43.5 us -> none  [block_least(): lax.dot_general(full_points, candidate, (((1,), (1,)), ((), ())), preferr...]
    scatter-add x2 -> x0, other arithmetic: 35.5 us -> none  [the longest x1 24.3 us: shards(): sums = jnp.zeros((list_count, half_width), jnp.float32).at[flat_index].ad...]
    ppermute x4 -> x0, starting transfers between devices: 31.3 us -> none  [passed_along(): return lax.ppermute(block, axis, route)]
    ppermute x4 -> x0, waiting for transfers between devices: 24.5 us -> none  [passed_along(): return lax.ppermute(block, axis, route)]
    convert_element_type x3 -> x0, other arithmetic: 22.2 us -> none  [the longest x1 12.4 us: shards(): centroids.astype(jnp.float32)]
    all_to_all x3 -> x0, starting transfers between devices: 20.4 us -> none  [the longest x1 7.32 us: shards(): lax.all_to_all(send_index.reshape(block_count, slot_count), 'blk', split_...]
  transfers between devices with their start and end apart: 8 -> 0, of which waited for: 4 -> 0; matrix products, arithmetic and copies ran while one was open for 34% -> 0% of each run, Pallas kernels for 0% -> 0%
where the time goes in v1:
time: 207 us; the launch traced here: 206 us
  Pallas kernels  198 us (96%)
  local copies, waits for them, and re-layouts  7.92 us (4%)
    pallas_call x1, Pallas kernels, shards(): pl.pallas_call(functools.partial(kernel, n, slots, tile), out_shape=(jax....  198 us
    unnamed x4, local copies, waits for them, and re-layouts  7.92 us

profile of v1, /device:TPU:1, one launch (start us, length us, event | category | flops | bytes accessed | tf_op | source)
XLA Modules:
  0.0 206.3 jit_solution(14558926674891670966)
XLA Ops:
  0.6 197.8 %shard_map.59 = (bf16[8192,512]{1,0:T(8,128)(2,1)}, f32[1,1024]{1,0:T(1,128)}) custom-call(s32[1,1024]{1,0:T(1,128)} %bitcast.3, s32[1,1024]{1,0:T(1,128)} %bitcast.4, bf16[1024,512]{1,0:T(8,128)(2,1)} %points_hbm.1, bf16[8192,512]{1,0:T(8,128)(2,1)} %cent_hbm.1), custom_call_target="tpu_custom_call" | custom-call | tf_op jit(solution)/shard_map/pallas_call | solution.py:254
  198.4 0.0 copy-start
  198.4 7.3 %copy.8 = bf16[8192,512]{1,0:T(8,128)(2,1)} copy(bf16[8192,512]{1,0:T(8,128)(2,1)} %get-tuple-element.8) | data formatting | bytes 16777216
  205.8 0.0 copy-done
  205.8 0.6 copy.9
Async XLA Ops:
  198.4 7.3 %copy-start = (f32[1,1024]{1,0:T(1,128)S(1)}, f32[1,1024]{1,0:T(1,128)}, u32[]{:S(2)}) copy-start(f32[1,1024]{1,0:T(1,128)} %get-tuple-element.5) | copy-start | bytes 12292

commit v2 on v1

--- a/solution.py
+++ b/solution.py
@@ -15,7 +15,7 @@
 
 
 def kernel(
-    n, slots, tile,
+    n, slots, units,
     owner_ref, member_ref, points_hbm, cent_hbm,
     new_hbm, near_ref,
     pts, cent, cand, send, recv, isend, irecv, idx_row, slot_row, mins, got, squares,
@@ -25,7 +25,8 @@
     rows, half = points_hbm.shape
     lists = cent_hbm.shape[0]
     keep = lists // 2
-    chunks = keep // tile
+    unit = keep // units
+    piece = unit // 2
     total = n * slots
     share = LANES // slots
     me, side = lax.axis_index("blk"), lax.axis_index("dim")
@@ -111,6 +112,20 @@
     irecv[me] = isend[me]
 
     point_copy.wait()
+    odd = lax.rem(me, 2) == 1
+
+    def ring(source, back, slot, sem):
+        return pltpu.make_async_remote_copy(
+            src_ref=pts.at[source], dst_ref=pts.at[slot],
+            send_sem=ring_send.at[sem], recv_sem=ring_recv.at[slot - 1],
+            device_id=(lax.rem(me + n - back, n), side), device_id_type=MESH)
+
+    to_one, to_two, handed = ring(0, 1, 1, 0), ring(0, 2, 2, 1), ring(1, 1, 2, 2)
+
+    @pl.when(odd)
+    def _():
+        to_one.start()
+
     ones = jnp.ones((8, 2 * half), BF16)
     block = min(256, rows)
     for r in range(rows // block):
@@ -137,77 +152,98 @@
             line = line + irecv[g * share + i]
         idx_row[:, g * LANES:(g + 1) * LANES] = line
 
-    previous = lax.rem(me + n - 1, n)
-
-    def ring(s):
-        return pltpu.make_async_remote_copy(
-            src_ref=pts.at[s - 1], dst_ref=pts.at[s],
-            send_sem=ring_send.at[s - 1], recv_sem=ring_recv.at[s - 1],
-            device_id=(previous, side), device_id_type=MESH)
-
-    ring(1).start()
-
-    def updated(first):
-        number = lax.broadcasted_iota(I32, (tile, total), 0) + (first + 1)
-        hot = (number == idx_row[0:1, :]).astype(F32)
+    @pl.when(odd)
+    def _():
+        to_two.start()
+
+    @pl.when(jnp.logical_not(odd))
+    def _():
+        to_one.start()
+
+    def updated(first, size):
+        wanted = idx_row[0:1, :] - (first + 1)
+        hot = (lax.broadcasted_iota(I32, (size, total), 0) == wanted).astype(F32)
         count = jnp.sum(hot, axis=1, keepdims=True)
         sums = jnp.dot(hot.astype(BF16), recv[...], preferred_element_type=F32)
-        old = cent[pl.ds(first, tile), :].astype(F32)
+        old = cent[pl.ds(first, size), :].astype(F32)
         return ((sums + old) * (1.0 / (count + 1.0))).astype(BF16)
 
-    def start_of(c, whose):
-        return pl.multiple_of(whose * keep + c * tile, tile)
-
-    def chunk_copy(c):
+    def at(start, size):
+        return pl.ds(pl.multiple_of(start, piece), size)
+
+    def chunk_copy(c, start, size):
         return pltpu.make_async_remote_copy(
-            src_ref=cent.at[pl.ds(start_of(c, other), tile)],
-            dst_ref=cand.at[pl.ds(pl.multiple_of(c * tile, tile), tile), pl.ds(half, half)],
+            src_ref=cent.at[at(other * keep + start, size)],
+            dst_ref=cand.at[at(start, size), pl.ds(half, half)],
             send_sem=chunk_send.at[c], recv_sem=chunk_recv.at[c],
             device_id=(me, other), device_id_type=MESH)
 
-    def sent_out(c):
-        place = pl.ds(start_of(c, other), tile)
+    def sent_out(c, start, size):
+        place = at(other * keep + start, size)
         return pltpu.make_async_copy(cent.at[place], new_hbm.at[place], out_sem.at[0, c])
 
-    def kept_out(c):
-        here = pl.ds(pl.multiple_of(c * tile, tile), tile)
+    def kept_out(u):
         return pltpu.make_async_copy(
-            cand.at[here, pl.ds(0, half)], new_hbm.at[pl.ds(start_of(c, side), tile)],
-            out_sem.at[1, c])
-
-    def give(c, carry):
-        first = start_of(c, other)
-        cent[pl.ds(first, tile), :] = updated(first)
-        chunk_copy(c).start()
-        sent_out(c).start()
-        return carry
-
-    lax.fori_loop(0, chunks, give, 0)
-    for s in range(1, CYCLE):
-        ring(s).wait_recv()
-        ring(s + 1).start()
-
-    def hold(c, carry):
-        here = pl.ds(pl.multiple_of(c * tile, tile), tile)
-        cand[here, 0:half] = updated(start_of(c, side))
-        kept_out(c).start()
-        return carry
-
-    lax.fori_loop(0, chunks, hold, 0)
-    ring(CYCLE).wait_recv()
-
-    def search(c, carry):
-        chunk_copy(c).wait_recv()
-        block_c = cand[pl.ds(pl.multiple_of(c * tile, tile), tile), :]
+            cand.at[at(u * unit, unit), pl.ds(0, half)],
+            new_hbm.at[at(side * keep + u * unit, unit)], out_sem.at[1, u])
+
+    def give(c, start, size):
+        first = pl.multiple_of(other * keep + start, piece)
+        cent[pl.ds(first, size), :] = updated(first, size)
+        chunk_copy(c, start, size).start()
+        sent_out(c, start, size).start()
+
+    last = (units - 1) * unit
+    ends = [(0, 0), (1, piece), (units, last), (units + 1, last + piece)]
+
+    def loop(low, high, body):
+        def step(u, carry):
+            body(u)
+            return carry
+        lax.fori_loop(low, high, step, 0)
+
+    def hold(u):
+        cand[at(u * unit, unit), 0:half] = updated(pl.multiple_of(side * keep + u * unit, unit), unit)
+        kept_out(u).start()
+
+    for c, start in ends[:2]:
+        give(c, start, piece)
+    loop(1, units - 1, lambda u: give(u + 1, u * unit, unit))
+    for c, start in ends[2:]:
+        give(c, start, piece)
+    loop(0, units, hold)
+
+    def search(start, size, sections):
+        block_c = cand[at(start, size), :]
         wide = block_c.astype(F32)
         half_square = 0.5 * jnp.sum(wide * wide, axis=1, keepdims=True)
-        for s in range(CYCLE + 1):
+        for s in sections:
             inner = lax.dot_general(block_c, pts[s], NT, preferred_element_type=F32)
-            value = (half_square - inner).reshape(tile // 8, 8, rows)
+            value = (half_square - inner).reshape(size // 8, 8, rows)
             mins[s] = jnp.minimum(mins[s], jnp.min(value, axis=0))
-        return carry
-
-    lax.fori_loop(0, chunks, search, 0)
+
+    def arrived(u, sections):
+        chunk_copy(u + 1, u * unit, unit).wait_recv()
+        search(u * unit, unit, sections)
+
+    for c, start in ends[:2]:
+        chunk_copy(c, start, piece).wait_recv()
+    search(0, unit, (0,))
+    loop(1, units // 2, lambda u: arrived(u, (0,)))
+    to_one.wait_recv()
+
+    @pl.when(odd)
+    def _():
+        handed.start()
+
+    loop(0, units // 2, lambda u: search(u * unit, unit, (1,)))
+    loop(units // 2, units - 2, lambda u: arrived(u, (0, 1)))
+    to_two.wait_recv()
+    loop(0, units - 2, lambda u: search(u * unit, unit, (2,)))
+    arrived(units - 2, range(CYCLE + 1))
+    for c, start in ends[2:]:
+        chunk_copy(c, start, piece).wait_recv()
+        search(start, piece, range(CYCLE + 1))
 
     back = []
     for s in range(CYCLE + 1):
@@ -221,15 +257,21 @@
     for copy in back:
         copy.start()
 
-    def finish(c, carry):
-        chunk_copy(c).wait_send()
-        sent_out(c).wait()
-        kept_out(c).wait()
-        return carry
-
-    lax.fori_loop(0, chunks, finish, 0)
-    for s in range(1, CYCLE + 1):
-        ring(s).wait_send()
+    def gone(c, start, size):
+        chunk_copy(c, start, size).wait_send()
+        sent_out(c, start, size).wait()
+
+    for c, start in ends:
+        gone(c, start, piece)
+    loop(1, units - 1, lambda u: gone(u + 1, u * unit, unit))
+    loop(0, units, lambda u: kept_out(u).wait())
+    to_one.wait_send()
+
+    @pl.when(odd)
+    def _():
+        to_two.wait_send()
+        handed.wait_send()
+
     for copy in back:
         copy.wait()
     best = mins[0]
@@ -246,13 +288,13 @@
     rows, half = points.shape
     lists = centroids.shape[0]
     slots = 2 * rows // n
-    tile = min(256, lists // 4)
-    chunks = lists // 2 // tile
+    units = 8
+    chunks = units + 2
     total = n * slots
     anywhere, vmem = pl.BlockSpec(memory_space=pl.ANY), pl.BlockSpec(memory_space=pltpu.VMEM)
     dma = pltpu.SemaphoreType.DMA
     new, near = pl.pallas_call(
-        functools.partial(kernel, n, slots, tile),
+        functools.partial(kernel, n, slots, units),
         out_shape=(
             jax.ShapeDtypeStruct(centroids.shape, BF16),
             jax.ShapeDtypeStruct((1, rows), F32),
@@ -273,7 +315,7 @@
             pltpu.VMEM((2, CYCLE + 1, 8, rows), F32),
             pltpu.VMEM((8, rows), F32),
             dma((2,)), dma((n,)), dma((n,)), dma((n,)), dma((n,)), dma, dma,
-            dma((CYCLE,)), dma((CYCLE,)), dma((chunks,)), dma((chunks,)), dma((2, chunks)),
+            dma((CYCLE + 1,)), dma((CYCLE,)), dma((chunks,)), dma((chunks,)), dma((2, chunks)),
             dma((2, CYCLE + 1)), dma((2, CYCLE + 1)),
         ],
         compiler_params=pltpu.CompilerParams(

time: 207 us -> 206 us (level)
  no operation moved by 1% of the time
where the time goes in v2:
time: 206 us
  Pallas kernels  198 us (96%)
  local copies, waits for them, and re-layouts  7.92 us (4%)
    pallas_call x1, Pallas kernels, shards(): pl.pallas_call(functools.partial(kernel, n, slots, units), out_shape=(jax...  198 us
    unnamed x4, local copies, waits for them, and re-layouts  7.92 us

profile of v2, /device:TPU:1, one launch (start us, length us, event | category | flops | bytes accessed | tf_op | source)
XLA Modules:
  0.0 206.2 jit_solution(4624111318809499516)
XLA Ops:
  0.6 197.6 %shard_map.59 = (bf16[8192,512]{1,0:T(8,128)(2,1)}, f32[1,1024]{1,0:T(1,128)}) custom-call(s32[1,1024]{1,0:T(1,128)} %bitcast.3, s32[1,1024]{1,0:T(1,128)} %bitcast.4, bf16[1024,512]{1,0:T(8,128)(2,1)} %points_hbm.1, bf16[8192,512]{1,0:T(8,128)(2,1)} %cent_hbm.1), custom_call_target="tpu_custom_call" | custom-call | tf_op jit(solution)/shard_map/pallas_call | solution.py:296
  198.2 0.0 copy-start
  198.3 7.3 %copy.8 = bf16[8192,512]{1,0:T(8,128)(2,1)} copy(bf16[8192,512]{1,0:T(8,128)(2,1)} %get-tuple-element.8) | data formatting | bytes 16777216
  205.6 0.0 copy-done
  205.6 0.6 copy.9
Async XLA Ops:
  198.2 7.3 %copy-start = (f32[1,1024]{1,0:T(1,128)S(1)}, f32[1,1024]{1,0:T(1,128)}, u32[]{:S(2)}) copy-start(f32[1,1024]{1,0:T(1,128)} %get-tuple-element.5) | copy-start | bytes 12292

commit v3 on v2

--- a/solution.py
+++ b/solution.py
@@ -98,7 +98,7 @@
         return row_copy, ind_copy
 
     def dispatch(i, carry):
-        d = 1 + lax.rem(i + n // 4, n - 1)
+        d = n // 2 + ((i + 1) // 2) * (1 - 2 * lax.rem(i, 2))
         base, packed = pack(lax.rem(me + d, n))
         send[pl.ds(base, slots), :] = packed
         row_copy, ind_copy = copies(d)
@@ -152,14 +152,6 @@
             line = line + irecv[g * share + i]
         idx_row[:, g * LANES:(g + 1) * LANES] = line
 
-    @pl.when(odd)
-    def _():
-        to_two.start()
-
-    @pl.when(jnp.logical_not(odd))
-    def _():
-        to_one.start()
-
     def updated(first, size):
         wanted = idx_row[0:1, :] - (first + 1)
         hot = (lax.broadcasted_iota(I32, (size, total), 0) == wanted).astype(F32)
@@ -211,6 +203,14 @@
     loop(1, units - 1, lambda u: give(u + 1, u * unit, unit))
     for c, start in ends[2:]:
         give(c, start, piece)
+    @pl.when(odd)
+    def _():
+        to_two.start()
+
+    @pl.when(jnp.logical_not(odd))
+    def _():
+        to_one.start()
+
     loop(0, units, hold)
 
     def search(start, size, sections):

time: 206 us -> 161 us (0.78); the launches traced: 206 us -> 159 us
  Pallas kernels: 198 us -> 150 us
    pallas_call x1, Pallas kernels: 198 us -> 150 us  [shards(): pl.pallas_call(functools.partial(kernel, n, slots, units), out_shape=(jax...]
where the time goes in v3:
time: 161 us; the launch traced here: 159 us
  Pallas kernels  150 us (93%)
  local copies, waits for them, and re-layouts  7.92 us (5%)
    pallas_call x1, Pallas kernels, shards(): pl.pallas_call(functools.partial(kernel, n, slots, units), out_shape=(jax...  150 us
    unnamed x4, local copies, waits for them, and re-layouts  7.92 us

profile of v3, /device:TPU:1, one launch (start us, length us, event | category | flops | bytes accessed | tf_op | source)
XLA Modules:
  0.0 158.9 jit_solution(3030117963097830208)
XLA Ops:
  0.6 150.3 %shard_map.59 = (bf16[8192,512]{1,0:T(8,128)(2,1)}, f32[1,1024]{1,0:T(1,128)}) custom-call(s32[1,1024]{1,0:T(1,128)} %bitcast.3, s32[1,1024]{1,0:T(1,128)} %bitcast.4, bf16[1024,512]{1,0:T(8,128)(2,1)} %points_hbm.1, bf16[8192,512]{1,0:T(8,128)(2,1)} %cent_hbm.1), custom_call_target="tpu_custom_call" | custom-call | tf_op jit(solution)/shard_map/pallas_call | solution.py:296
  151.0 0.0 copy-start
  151.0 7.3 %copy.8 = bf16[8192,512]{1,0:T(8,128)(2,1)} copy(bf16[8192,512]{1,0:T(8,128)(2,1)} %get-tuple-element.8) | data formatting | bytes 16777216
  158.3 0.0 copy-done
  158.3 0.6 copy.9
Async XLA Ops:
  151.0 7.3 %copy-start = (f32[1,1024]{1,0:T(1,128)S(1)}, f32[1,1024]{1,0:T(1,128)}, u32[]{:S(2)}) copy-start(f32[1,1024]{1,0:T(1,128)} %get-tuple-element.5) | copy-start | bytes 12292
